TPU v7x, 32 devices: a whole 2x2x4 slice. The times are simulated.
32 devices in a mesh: dp: 8 (over z, y), seq: 4 (over x, core).
Axes of the slice: x: 2, y: 2, z: 4, core: 2. Of those that a mesh axis runs over, the one named last changes fastest.
Arguments:
- acts: bfloat16 [16, 512, 4608], P('dp', 'seq'), may hold values from -20 to 20, as said below
- grads: bfloat16 [16, 512, 18432], P('dp', 'seq'), may hold values from -0.00045670236 to 0.00045670236, as said below
Outputs:
- update: bfloat16 [4608, 18432], P('dp', 'seq')
- norms: float32 [16], P('dp')
Inputs may be any that keep to these rules, and one draw needn't show every extreme that they name: `acts`: entries of order one. `grads`: independent entries, small: magnitudes under 2000 / (21 * sqrt(43486543872)).
All inputs are finite; a program needn't handle non-finite values.
Results may differ from a plain program's by a relative error of at most 0.025.
Values may be sent and summed in bfloat16 or wider, within the bound.
A program may use at most 192 MiB of HBM per device.

v0:
```python
import math

import jax
import jax.numpy as jnp
from jax import lax
from jax.sharding import PartitionSpec as P


def on_device(acts, grads):
    seq_count = lax.axis_size("seq")
    replica_count = lax.axis_size("dp")
    examples, local_len, width = acts.shape
    hidden = grads.shape[2]
    complete_matrix = lax.all_gather(acts, "seq", axis=1, tiled=True)
    column_total = lax.all_to_all(grads, "seq", split_axis=2, concat_axis=1, tiled=True)
    gradient_gram_matrix = jnp.einsum(
        "slf,smf->slm", column_total, column_total, preferred_element_type=jnp.float32
    )
    activation_gram_matrix = jnp.einsum(
        "nih,nfh->nif", complete_matrix, complete_matrix, preferred_element_type=jnp.float32
    )
    partial_value = jnp.sum(activation_gram_matrix * gradient_gram_matrix, axis=(1, 2))
    squared = lax.psum(partial_value, "seq")
    norms = jnp.sqrt(squared)
    clip = jnp.minimum(1.0, 1.0 / (norms + 1e-06))
    factor = math.sqrt(width * hidden / (examples * replica_count))
    scaled = (column_total * (clip * factor)[:, None, None]).astype(jnp.bfloat16)
    flat_acts = complete_matrix.reshape(-1, width)
    flat_scaled = scaled.reshape(-1, hidden // seq_count)
    total = lax.psum_scatter(
        lax.dot_general(
            flat_acts, flat_scaled, (((0,), (0,)), ((), ())), preferred_element_type=jnp.float32
        ).astype(jnp.bfloat16),
        "dp",
        scatter_dimension=0,
        tiled=True,
    )
    return (total, norms)


def solution(mesh):
    return jax.shard_map(
        on_device,
        mesh=mesh,
        in_specs=(P("dp", "seq", None), P("dp", "seq", None)),
        out_specs=(P("dp", "seq"), P("dp")),
        check_vma=False,
    )
```

profile of v0, /device:TPU:0, one launch (start us, length us, event | category | flops | bytes accessed | tf_op | source)
XLA Modules:
  0.0 1011.4 jit_solution(10249000364304703452)
XLA Ops:
  7.2 0.0 all-gather.2.cloned.1.call-start
  7.2 0.7 all-gather.2.cloned.1.call-update
  7.9 0.0 reduce-scatter.4.cloned.1.call-start
  7.9 24.0 %copy.7 = bf16[2,128,18432]{1,0,2:T(2,128)(2,1)} copy(bf16[2,128,18432]{2,1,0:T(8,128)(2,1)} %param.3) | data formatting | bytes 18874368 | tf_op args[1]
  31.9 144.0 %all_to_all.18 = bf16[2,128,18432]{1,0,2:T(2,128)(2,1)} all-to-all(bf16[2,128,18432]{1,0,2:T(2,128)(2,1)} %copy.7), channel_id=1, replica_groups=mesh['dp'=8,'seq'=4] {'seq'}, dimensions={2} | all-to-all | bytes 18874368 | tf_op jit(solution)/shard_map/all_to_all | solution.py:15
  175.9 23.8 %copy.8 = bf16[2,128,4,4608]{3,1,2,0:T(8,128)(2,1)} copy(bf16[2,128,4,4608]{1,0,3,2:T(2,128)(2,1)} %bitcast.19) | data formatting | bytes 18874368 | tf_op jit(solution)/shard_map/all_to_all | solution.py:15
  199.7 0.0 all-gather.2.cloned.1.call-done
  199.7 0.0 copy-start
  199.7 10.5 %fusion.2 = f32[2,512,512]{2,1,0:T(8,128)S(1)} fusion(bf16[2,512,4608]{2,1,0:T(8,128)(2,1)} %all-gather.2.cloned.1.call-done), kind=kOutput, calls=%fused_computation.6 | convolution fusion | flops 4831838208 | bytes 11534336 | tf_op jit(solution)/shard_map/nih,nfh->nif/dot_general | solution.py:19
  210.2 0.0 copy-done
  210.3 5.3 multiply_reduce_fusion
  215.6 5.9 psum.7
  221.5 0.5 minimum_multiply_fusion
  222.0 53.8 %fusion = bf16[4608,4608]{0,1:T(8,128)(2,1)} fusion(bf16[2,512,4608]{2,1,0:T(8,128)(2,1)} %all-gather.2.cloned.1.call-done, bf16[2,512,4608]{2,1,0:T(8,128)(2,1)} %bitcast.20, f32[2]{0:T(128)S(1)} %get-tuple-element.6), kind=kOutput, calls=%fused_computation.1 | convolution fusion | flops 43521933312 | bytes 61341704 | tf_op jit(solution)/shard_map/dot_general | solution.py:31
  275.8 54.6 %copy.12 = bf16[4608,4608]{1,0:T(8,128)(2,1)} copy(bf16[4608,4608]{0,1:T(8,128)(2,1)} %fusion) | data formatting | bytes 84934656
  330.4 0.0 reduce-scatter.4.cloned.1.call-update
  330.4 674.1 %reduce-scatter.4.cloned.1.call-done = bf16[576,4608]{1,0:T(8,128)(2,1)} async-done(((bf16[4608,4608]{1,0:T(8,128)(2,1)}), bf16[576,4608]{1,0:T(8,128)(2,1)}) %reduce-scatter.4.cloned.1.call-update) | async-done | bytes 5308432
Async XLA Ops:
  7.2 192.5 %all-gather.2.cloned.1.call-start = ((), (), s32[]{:S(2)}) async-start(), calls=%async_computation.2 | async-start | bytes 11796480 | tf_op jit(solution)/shard_map/all_gather | solution.py:14
  7.9 996.7 %reduce-scatter.4.cloned.1.call-start = ((), (), s32[]{:S(2)}) async-start(), calls=%async_computation.3 | async-start | bytes 47775744
  199.7 10.5 %copy-start = (bf16[2,128,4,4608]{3,1,2,0:T(8,128)(2,1)S(1)}, bf16[2,128,4,4608]{3,1,2,0:T(8,128)(2,1)}, u32[]{:S(2)}) copy-start(bf16[2,128,4,4608]{3,1,2,0:T(8,128)(2,1)} %copy.8) | copy-start | bytes 28311556
Sparse Core Ops, SparseCore 0:
  9.6 97.9 all-gather.1
  330.5 673.9 reduce-scatter.3
where the time goes:
time: 1010 us
  waiting for transfers between devices  675 us (67%)
  blocking collectives  150 us (15%)
  local copies, waits for them, and re-layouts  102 us (10%)
  matrix products  69.6 us (7%)
  between operations  14.1 us (1%)
    unnamed x3, waiting for transfers between devices  675 us
    all_to_all x1, blocking collectives, on_device(): lax.all_to_all(grads, 'seq', split_axis=2, concat_axis=1, tiled=True)  144 us
    unnamed x4, local copies, waits for them, and re-layouts  78.6 us
    dot_general x1, matrix products, on_device(): lax.dot_general(flat_acts, flat_scaled, (((0,), (0,)), ((), ())), preferr...  53.8 us
    all_to_all x1, local copies, waits for them, and re-layouts, on_device(): lax.all_to_all(grads, 'seq', split_axis=2, concat_axis=1, tiled=True)  23.8 us
  transfers between devices with their start and end apart: 2, of which 1 were waited for; matrix products, arithmetic and copies ran while one was open for 5% of the time, Pallas kernels for 0%

commit v1 on v0

v1 whole, which is shorter than its diff:
```python
import functools
import math

import jax
import jax.numpy as jnp
from jax import lax
from jax.experimental import pallas as pl
from jax.experimental.pallas import tpu as pltpu
from jax.sharding import PartitionSpec as P

MESH = pl.DeviceIdType.MESH
PARTS = 3


def flip(value, bit):
    return value + bit * (1 - 2 * ((value // bit) % 2))


def xor(value, mask):
    bit = 1
    while bit <= mask:
        if mask & bit:
            value = flip(value, bit)
        bit *= 2
    return value


def powers(count, first):
    found, bit = [], 1
    while bit < count:
        found.append(bit * first)
        bit *= 2
    return found


def split_of(dp, seq, hidden):
    lanes = dp // 2
    while (hidden // seq) % (lanes * 128):
        lanes //= 2
    return lanes


def gather_kernel(L, seq, acts, grads, a_all, b_all,
                  a_send, a_recv, f_send, f_recv, b_send, b_recv, own_sem):
    d, s = lax.axis_index("dp"), lax.axis_index("seq")
    h, l = d // L, d % L
    E, T, D = acts.shape
    nb = b_all.shape[2]
    W = D // PARTS
    bits = [("s", m) for m in powers(seq // 2, 2)] + [("l", m) for m in powers(L, 1)]
    n = len(bits)
    blocks = 1 << n

    def relative(mask, order, core=0):
        ll, ss = l, s
        for j in range(n):
            if mask >> j & 1:
                kind, m = order[j]
                if kind == "s":
                    ss = flip(ss, m)
                else:
                    ll = flip(ll, m)
        if core:
            ss = flip(ss, 1)
        return ll, ss

    barrier = pltpu.get_barrier_semaphore()
    for mask in range(blocks):
        for core in range(2):
            if mask or core:
                ll, ss = relative(mask, bits, core)
                pl.semaphore_signal(barrier, inc=1, device_id=(h * L + ll, ss), device_id_type=MESH)
    pl.semaphore_wait(barrier, 2 * blocks - 1)

    def a_at(ll, ss, r):
        return a_all.at[pl.ds(ll * E, E), pl.ds(ss * T, T), pl.ds(r * W, W)]

    def order_of(r):
        return bits[r % n:] + bits[:r % n]

    def a_copy(r, mask, k):
        order = order_of(r)
        src = acts.at[:, :, pl.ds(r * W, W)] if mask == 0 else a_at(*relative(mask, order), r)
        tl, ts = relative(1 << k, order)
        land = mask | 1 << k
        return pltpu.make_async_remote_copy(
            src_ref=src, dst_ref=a_at(*relative(mask, order), r),
            send_sem=a_send.at[r, land], recv_sem=a_recv.at[r, land],
            device_id=(h * L + tl, ts), device_id_type=MESH)

    def f_copy(r, mask):
        order = order_of(r)
        src = acts.at[:, :, pl.ds(r * W, W)] if mask == 0 else a_at(*relative(mask, order), r)
        tl, ts = relative(0, order, 1)
        return pltpu.make_async_remote_copy(
            src_ref=src, dst_ref=a_at(*relative(mask, order), r),
            send_sem=f_send.at[r, mask], recv_sem=f_recv.at[r, mask],
            device_id=(h * L + tl, ts), device_id_type=MESH)

    def landed(ref, sems, *index):
        return pltpu.make_async_remote_copy(
            src_ref=ref, dst_ref=ref, send_sem=sems.at[index], recv_sem=sems.at[index],
            device_id=(d, s), device_id_type=MESH)

    def b_copy(mask, core):
        tl, ts = relative(mask, bits, core)
        column = pl.multiple_of((ts * L + tl) * nb, 128)
        return pltpu.make_async_remote_copy(
            src_ref=grads.at[:, :, pl.ds(column, nb)],
            dst_ref=b_all.at[pl.ds(l * E, E), pl.ds(s * T, T), :],
            send_sem=b_send.at[mask, core], recv_sem=b_recv.at[mask, core],
            device_id=(h * L + tl, ts), device_id_type=MESH)

    started = []

    def go(copy):
        copy.start()
        started.append(copy)

    for k in range(n):
        for r in range(PARTS):
            go(a_copy(r, 0, k))
    own_a = pltpu.make_async_copy(
        acts, a_all.at[pl.ds(l * E, E), pl.ds(s * T, T), :], own_sem.at[0])
    own_a.start()
    column = pl.multiple_of((s * L + l) * nb, 128)
    own_b = pltpu.make_async_copy(
        grads.at[:, :, pl.ds(column, nb)],
        b_all.at[pl.ds(l * E, E), pl.ds(s * T, T), :], own_sem.at[1])
    own_b.start()
    for r in range(PARTS):
        go(f_copy(r, 0))
    to_send = sorted(
        ((m, c) for m in range(blocks) for c in range(2) if m or c),
        key=lambda mc: -bin(mc[0]).count("1"))
    half = len(to_send) // 2
    for mc in to_send[:half]:
        go(b_copy(*mc))
    arrivals = sorted(range(1, blocks), key=lambda m: (bin(m).count("1"), m))
    seen = 0
    for mask in arrivals:
        for r in range(PARTS):
            order = order_of(r)
            landed(a_at(*relative(mask, order), r), a_recv, r, mask).wait_recv()
            for k in range(mask.bit_length(), n):
                go(a_copy(r, mask, k))
            go(f_copy(r, mask))
        seen += 1
        if seen == n:
            for mc in to_send[half:]:
                go(b_copy(*mc))
    if seen < n:
        for mc in to_send[half:]:
            go(b_copy(*mc))
    for r in range(PARTS):
        order = order_of(r)
        for mask in range(blocks):
            landed(a_at(*relative(mask, order, 1), r), f_recv, r, mask).wait_recv()
    for mask, core in to_send:
        ll, ss = relative(mask, bits, core)
        landed(b_all.at[pl.ds(ll * E, E), pl.ds(ss * T, T), :], b_recv, mask, core).wait_recv()
    for copy in started:
        copy.wait_send()
    own_a.wait()
    own_b.wait()


def gather(L, seq, acts, grads):
    E, T, D = acts.shape
    nb = grads.shape[2] // (seq * L)
    blocks = L * seq // 2
    dma = pltpu.SemaphoreType.DMA
    return pl.pallas_call(
        functools.partial(gather_kernel, L, seq),
        out_shape=(
            jax.ShapeDtypeStruct((L * E, seq * T, D), acts.dtype),
            jax.ShapeDtypeStruct((L * E, seq * T, nb), grads.dtype),
        ),
        in_specs=[pl.BlockSpec(memory_space=pl.ANY)] * 2,
        out_specs=(pl.BlockSpec(memory_space=pl.ANY),) * 2,
        scratch_shapes=[
            dma((PARTS, blocks)), dma((PARTS, blocks)),
            dma((PARTS, blocks)), dma((PARTS, blocks)),
            dma((blocks, 2)), dma((blocks, 2)), dma((2,)),
        ],
        compiler_params=pltpu.CompilerParams(collective_id=0, has_side_effects=True),
        name="gather_tokens",
    )(acts, grads)


def product_kernel(H, L, RB, TM, a_ref, b_ref, out, a_buf, b_buf, c_buf, recv,
                   a_sem, b_sem, s_send, s_recv, o_send, o_recv, own_sem):
    d, s = lax.axis_index("dp"), lax.axis_index("seq")
    h, l = d // L, d % L
    K, D = a_ref.shape
    nb = b_ref.shape[1]
    tiles, k = D // TM, TM // RB
    b_load = pltpu.make_async_copy(b_ref, b_buf, b_sem)
    b_load.start()
    whole_tiles = L % k == 0
    plan = []
    if whole_tiles:
        per = L // k
        for o in list(range(1, H)) + [0]:
            hh = (h + o) % H
            for i in reversed(range(per)):
                tile = hh * per + xor(l // k, i)
                plan.append((tile, [(tile * k + xor(l % k, j), o != 0) for j in reversed(range(k))]))
    else:
        first = (h + 1) * L // k
        for i in range(tiles):
            tile = (first + i) % tiles
            plan.append((tile, [(tile * k + j, None) for j in range(k)]))

    def a_load(i):
        column = pl.multiple_of(plan[i][0] * TM, 128)
        return pltpu.make_async_copy(a_ref.at[:, pl.ds(column, TM)], a_buf.at[i % 2], a_sem.at[i % 2])

    a_load(0).start()
    barrier = pltpu.get_barrier_semaphore()
    for o in range(1, H):
        pl.semaphore_signal(barrier, inc=1, device_id=((h + o) % H * L + l, s), device_id_type=MESH)
    for i in range(1, L):
        pl.semaphore_signal(barrier, inc=1, device_id=(h * L + xor(l, i), s), device_id_type=MESH)
    pl.semaphore_wait(barrier, H + L - 2)

    def s_copy(block):
        hh, ll = block // L, block % L
        slot = (h - hh + H) % H - 1
        return pltpu.make_async_remote_copy(
            src_ref=c_buf.at[pl.ds(pl.multiple_of(block * RB, 16), RB)],
            dst_ref=recv.at[slot, pl.ds(pl.multiple_of(ll * RB, 16), RB)],
            send_sem=s_send.at[block], recv_sem=s_recv.at[slot, ll],
            device_id=(hh * L + l, s), device_id_type=MESH)

    chunk = 384
    for i, (tile, rows) in enumerate(plan):
        if i + 1 < tiles:
            a_load(i + 1).start()
        a_load(i).wait()
        if i == 0:
            b_load.wait()

        @pl.loop(0, TM // chunk)
        def _(m):
            column = pl.multiple_of(m * chunk, 128)
            value = lax.dot_general(
                a_buf[i % 2, :, pl.ds(column, chunk)], b_buf[...],
                (((0,), (0,)), ((), ())), preferred_element_type=jnp.float32)
            row = pl.multiple_of(tile * TM + m * chunk, 128)
            c_buf[pl.ds(row, chunk), :] = value.astype(jnp.bfloat16)

        for block, away in rows:
            if away is None:
                @pl.when(block // L != h)
                def _():
                    s_copy(block).start()
            elif away:
                s_copy(block).start()

    def o_copy(i):
        ll = xor(l, i)
        src = c_buf.at[pl.ds(pl.multiple_of((h * L + ll) * RB, 16), RB)]
        return pltpu.make_async_remote_copy(
            src_ref=src, dst_ref=out.at[:, pl.ds(pl.multiple_of(l * nb, 128), nb)],
            send_sem=o_send.at[i], recv_sem=o_recv.at[i],
            device_id=(h * L + ll, s), device_id_type=MESH)

    own = pltpu.make_async_copy(
        c_buf.at[pl.ds(pl.multiple_of((h * L + l) * RB, 16), RB)],
        out.at[:, pl.ds(pl.multiple_of(l * nb, 128), nb)], own_sem)
    step = 96
    for i in reversed(range(L)):
        ll = xor(l, i)
        for slot in range(H - 1):
            land = recv.at[slot, pl.ds(pl.multiple_of(ll * RB, 16), RB)]
            pltpu.make_async_remote_copy(
                src_ref=land, dst_ref=land, send_sem=s_recv.at[slot, ll],
                recv_sem=s_recv.at[slot, ll], device_id=(d, s), device_id_type=MESH).wait_recv()

        @pl.loop(0, RB // step)
        def _(m):
            here = pl.ds(pl.multiple_of((h * L + ll) * RB + m * step, 16), step)
            there = pl.ds(pl.multiple_of(ll * RB + m * step, 16), step)
            total = c_buf[here, :].astype(jnp.float32)
            for slot in range(H - 1):
                total = total + recv[slot, there, :].astype(jnp.float32)
            c_buf[here, :] = total.astype(jnp.bfloat16)

        if i:
            o_copy(i).start()
        else:
            own.start()
    for o in range(1, H):
        for ll in range(L):
            s_copy((h + o) % H * L + ll).wait_send()
    for i in range(1, L):
        land = out.at[:, pl.ds(pl.multiple_of(xor(l, i) * nb, 128), nb)]
        pltpu.make_async_remote_copy(
            src_ref=land, dst_ref=land, send_sem=o_recv.at[i], recv_sem=o_recv.at[i],
            device_id=(d, s), device_id_type=MESH).wait_recv()
        o_copy(i).wait_send()
    own.wait()


def product(dp, seq, L, a_all, b_all):
    K, D = a_all.shape
    nb = b_all.shape[1]
    H, RB = dp // L, D // dp
    TM = math.lcm(RB, 128)
    dma = pltpu.SemaphoreType.DMA
    return pl.pallas_call(
        functools.partial(product_kernel, H, L, RB, TM),
        out_shape=jax.ShapeDtypeStruct((RB, nb * L), jnp.bfloat16),
        in_specs=[pl.BlockSpec(memory_space=pl.ANY)] * 2,
        out_specs=pl.BlockSpec(memory_space=pl.ANY),
        scratch_shapes=[
            pltpu.VMEM((2, K, TM), jnp.bfloat16),
            pltpu.VMEM((K, nb), jnp.bfloat16),
            pltpu.VMEM((D, nb), jnp.bfloat16),
            pltpu.VMEM((H - 1, L * RB, nb), jnp.bfloat16),
            dma((2,)), dma, dma((dp,)), dma((H - 1, L)), dma((L,)), dma((L,)), dma,
        ],
        compiler_params=pltpu.CompilerParams(
            collective_id=1, has_side_effects=True, vmem_limit_bytes=60 * 2**20),
        cost_estimate=pl.CostEstimate(
            flops=2 * K * D * nb, bytes_accessed=2 * (K * D + K * nb + RB * nb * L), transcendentals=0),
        name="product_scatter",
    )(a_all, b_all)


def on_device(acts, grads):
    seq, dp = lax.axis_size("seq"), lax.axis_size("dp")
    examples, local_len, width = acts.shape
    hidden = grads.shape[2]
    L = split_of(dp, seq, hidden)
    d = lax.axis_index("dp")
    a_all, b_all = gather(L, seq, acts, grads)
    act_gram = jnp.einsum("nih,nfh->nif", a_all, a_all, preferred_element_type=jnp.float32)
    grad_gram = jnp.einsum("nih,nfh->nif", b_all, b_all, preferred_element_type=jnp.float32)
    part = jnp.sum(act_gram * grad_gram, axis=(1, 2))
    here = d // L * (L * examples)
    every = lax.dynamic_update_slice(jnp.zeros((dp * examples,), jnp.float32), part, (here,))
    norms = jnp.sqrt(lax.psum(every, ("dp", "seq")))
    clip = jnp.minimum(1.0, 1.0 / (norms + 1e-06))
    factor = math.sqrt(width * hidden / (examples * dp))
    scale = lax.dynamic_slice(clip * factor, (here,), (L * examples,))
    scaled = (b_all * scale[:, None, None]).astype(jnp.bfloat16)
    tokens = L * examples * seq * local_len
    update = product(dp, seq, L, a_all.reshape(tokens, width), scaled.reshape(tokens, -1))
    return update, lax.dynamic_slice(norms, (d * examples,), (examples,))


def solution(mesh):
    return jax.shard_map(
        on_device,
        mesh=mesh,
        in_specs=(P("dp", "seq", None), P("dp", "seq", None)),
        out_specs=(P("dp", "seq"), P("dp")),
        check_vma=False,
    )
```

time: 1010 us -> 596 us (0.59)
  waiting for transfers between devices: 675 us -> 0 us
  Pallas kernels: 0 us -> 494 us
  blocking collectives: 150 us -> 39.6 us
  local copies, waits for them, and re-layouts: 102 us -> 6.1 us
  matrix products: 69.6 us -> 45.6 us
  between operations: 14.1 us -> 0.67 us
    unnamed x3 -> x0, waiting for transfers between devices: 675 us -> none
    pallas_call x0 -> x2, Pallas kernels: none -> 494 us  [the longest x1 252 us: product(): pl.pallas_call(functools.partial(product_kernel, H, L, RB, TM), out_shape...]
    all_to_all x1 -> x0, blocking collectives: 144 us -> none  [on_device(): lax.all_to_all(grads, 'seq', split_axis=2, concat_axis=1, tiled=True)]
    unnamed x4 -> x1, local copies, waits for them, and re-layouts: 78.6 us -> 5.23 us
    psum x1, blocking collectives: 5.91 us -> 39.6 us  [on_device(): norms = jnp.sqrt(lax.psum(every, ('dp', 'seq')))]
    dot_general x3 -> x2, matrix products: 69.6 us -> 45.6 us  [the longest x1 32.7 us: on_device(): jnp.einsum('nih,nfh->nif', a_all, a_all, preferred_element_type=jnp.float32)]
    all_to_all x1 -> x0, local copies, waits for them, and re-layouts: 23.8 us -> none  [on_device(): lax.all_to_all(grads, 'seq', split_axis=2, concat_axis=1, tiled=True)]
  transfers between devices with their start and end apart: 2 -> 0, of which waited for: 1 -> 0; matrix products, arithmetic and copies ran while one was open for 5% -> 0% of each run, Pallas kernels for 0% -> 0%
where the time goes in v1:
time: 596 us
  Pallas kernels  494 us (83%)
  matrix products  45.6 us (8%)
  blocking collectives  39.6 us (7%)
  other arithmetic  9.87 us (2%)
  local copies, waits for them, and re-layouts  6.1 us (1%)
    pallas_call x1, Pallas kernels, product(): pl.pallas_call(functools.partial(product_kernel, H, L, RB, TM), out_shape...  252 us
    pallas_call x1, Pallas kernels, gather(): pl.pallas_call(functools.partial(gather_kernel, L, seq), out_shape=(jax.S...  243 us
    psum x1, blocking collectives, on_device(): norms = jnp.sqrt(lax.psum(every, ('dp', 'seq')))  39.6 us
    dot_general x1, matrix products, on_device(): jnp.einsum('nih,nfh->nif', a_all, a_all, preferred_element_type=jnp.float32)  32.7 us
    dot_general x1, matrix products, on_device(): jnp.einsum('nih,nfh->nif', b_all, b_all, preferred_element_type=jnp.float32)  13 us

profile of v1, /device:TPU:0, one launch (start us, length us, event | category | flops | bytes accessed | tf_op | source)
XLA Modules:
  0.0 596.1 jit_solution(18085781100956470208)
XLA Ops:
  0.7 242.7 %gather_tokens.1 = (bf16[8,512,4608]{2,1,0:T(8,128)(2,1)}, bf16[8,512,1152]{2,1,0:T(8,128)(2,1)}) custom-call(bf16[2,128,4608]{2,1,0:T(8,128)(2,1)} %acts.1, bf16[2,128,18432]{2,1,0:T(8,128)(2,1)} %grads.1), custom_call_target="tpu_custom_call" | custom-call | tf_op jit(solution)/shard_map/gather_tokens/pallas_call | solution.py:173
  243.3 13.0 %fusion.1 = f32[8,512,512]{2,1,0:T(8,128)} fusion(bf16[8,512,1152]{2,1,0:T(8,128)(2,1)} %get-tuple-element.5), kind=kOutput, calls=%fused_computation.4 | convolution fusion | flops 4831838208 | bytes 17825792 | tf_op jit(solution)/shard_map/nih,nfh->nif/dot_general | solution.py:340
  256.3 32.7 %multiply_reduce_fusion = f32[8]{0:T(128)S(1)} fusion(f32[8,512,512]{2,1,0:T(8,128)} %fusion.1, bf16[8,512,4608]{2,1,0:T(8,128)(2,1)} %get-tuple-element.4), kind=kOutput, calls=%fused_computation.1 | convolution fusion | flops 19331547136 | bytes 46137376 | tf_op jit(solution)/shard_map/nih,nfh->nif/dot_general | solution.py:339
  289.0 0.2 dynamic_update_slice.3
  289.2 39.6 %psum.7 = f32[16]{0:T(128)S(1)} all-reduce(f32[16]{0:T(128)S(1)} %dynamic_update_slice.3), channel_id=1, replica_groups=mesh['dp'=8,'seq'=4] {'dp','seq'}, use_global_device_ids=true, to_apply=%region_1.2 | all-reduce | flops 16 | bytes 128 | tf_op jit(solution)/shard_map/psum | solution.py:344
  328.8 0.6 dynamic_slice.7
  329.4 0.1 dynamic_slice.6
  329.5 9.9 %multiply_convert_fusion = bf16[8,512,1152]{2,1,0:T(8,128)(2,1)} fusion(bf16[8,512,1152]{2,1,0:T(8,128)(2,1)} %get-tuple-element.5, f32[8]{0:T(128)S(1)} %dynamic_slice.6), kind=kLoop, calls=%fused_computation | loop fusion | flops 14155776 | bytes 18874400 | tf_op jit(solution)/shard_map/convert_element_type | solution.py:348
  339.3 251.5 %product_scatter.1 = bf16[576,4608]{1,0:T(8,128)(2,1)} custom-call(bf16[4096,4608]{1,0:T(8,128)(2,1)} %bitcast.7, bf16[4096,1152]{1,0:T(8,128)(2,1)} %bitcast.6), custom_call_target="tpu_custom_call" | custom-call | flops 43486543872 | bytes 52494336 | tf_op jit(solution)/shard_map/product_scatter/pallas_call | solution.py:312
  590.9 5.2 copy.6
  (2 shorter events, 0.0 us)

commit v2 on v0

v2 whole, which is shorter than its diff:
```python
import functools
import math

import jax
import jax.numpy as jnp
from jax import lax
from jax.experimental import pallas as pl
from jax.experimental.pallas import tpu as pltpu
from jax.sharding import PartitionSpec as P

MESH = pl.DeviceIdType.MESH


def flip(value, bit):
    return value + bit * (1 - 2 * ((value // bit) % 2))


def xor(value, mask):
    bit = 1
    while bit <= mask:
        if mask & bit:
            value = flip(value, bit)
        bit *= 2
    return value


def split_of(dp, seq, hidden):
    lanes = dp // 2
    while (hidden // seq) % (lanes * 128):
        lanes //= 2
    return lanes


def steps_of(H, L, RB, TM, D, h):
    tiles, k = D // TM, TM // RB
    first = (h + 1) * L // k
    return [(first + i) % tiles for i in range(tiles)]


def leader(l, c, n, mask):
    mirrored = sum(1 << (n - 1 - j) for j in range(n) if mask >> j & 1)
    return (1 - c) * xor(l, mask) + c * xor(l, mirrored)


def landed(ref, sem, d, s):
    return pltpu.make_async_remote_copy(
        src_ref=ref, dst_ref=ref, send_sem=sem, recv_sem=sem, device_id=(d, s), device_id_type=MESH)


class Spread:
    def __init__(self, h, l, s, L, own, buf, sems, copies):
        self.h, self.l, self.s, self.c, self.L = h, l, s, s % 2, L
        self.n = L.bit_length() - 1
        self.own, self.buf, self.copies = own, buf, copies
        self.t_send, self.t_recv, self.f_send, self.f_recv, self.local_sem = sems

    def at(self, ll, core):
        return self.buf.at[2 * ll + core]

    def send(self, mask, k):
        ll = leader(self.l, self.c, self.n, mask)
        land = mask | 1 << k
        copy = pltpu.make_async_remote_copy(
            src_ref=self.at(ll, self.c) if mask else self.own(self.c), dst_ref=self.at(ll, self.c),
            send_sem=self.t_send.at[land], recv_sem=self.t_recv.at[land],
            device_id=(self.h * self.L + leader(self.l, self.c, self.n, 1 << k), self.s),
            device_id_type=MESH)
        copy.start()
        self.copies.append(copy)

    def begin(self):
        for k in range(self.n):
            self.send(0, k)
        self.local = []
        for e in range(2):
            copy = pltpu.make_async_copy(self.own(e), self.at(self.l, e), self.local_sem.at[e])
            copy.start()
            self.local.append(copy)

    def forward(self):
        d = self.h * self.L + self.l
        for mask in sorted(range(1, 1 << self.n), key=lambda m: (bin(m).count("1"), m)):
            ll = leader(self.l, self.c, self.n, mask)
            here = self.at(ll, self.c)
            landed(here, self.t_recv.at[mask], d, self.s).wait_recv()
            for k in range(mask.bit_length(), self.n):
                self.send(mask, k)
            copy = pltpu.make_async_remote_copy(
                src_ref=here, dst_ref=here, send_sem=self.f_send.at[mask], recv_sem=self.f_recv.at[mask],
                device_id=(d, flip(self.s, 1)), device_id_type=MESH)
            copy.start()
            self.copies.append(copy)

    def finish(self):
        d = self.h * self.L + self.l
        for mask in range(1, 1 << self.n):
            ll = leader(self.l, 1 - self.c, self.n, mask)
            landed(self.at(ll, 1 - self.c), self.f_recv.at[mask], d, self.s).wait_recv()
        for copy in self.local:
            copy.wait()


def gather_kernel(H, L, seq, RB, TM, acts, grads, a_own, a_first, b_own, b_all,
                  a_send, a_recv, f_send, f_recv, b1_send, b1_recv, b2_send, b2_recv,
                  t_send, t_recv, tf_send, tf_recv, local_sem, own_sem):
    d, s = lax.axis_index("dp"), lax.axis_index("seq")
    h, l = d // L, d % L
    E, T, D = acts.shape
    nb = b_all.shape[2]
    tiles = steps_of(H, L, RB, TM, D, h)
    barrier = pltpu.get_barrier_semaphore()
    for q in range(1, seq):
        pl.semaphore_signal(barrier, inc=1, device_id=(d, xor(s, q)), device_id_type=MESH)
    for j in range(1, L):
        pl.semaphore_signal(barrier, inc=1, device_id=(h * L + xor(l, j), s), device_id_type=MESH)
    pl.semaphore_wait(barrier, seq + L - 2)

    copies = []

    def go(src, dst, send_sem, recv_sem, device):
        copy = pltpu.make_async_remote_copy(
            src_ref=src, dst_ref=dst, send_sem=send_sem, recv_sem=recv_sem,
            device_id=device, device_id_type=MESH)
        copy.start()
        copies.append(copy)

    def a_cols(i):
        return pl.ds(pl.multiple_of(tiles[i] * TM, 128), TM)

    def a_at(ss, i):
        return a_own.at[:, pl.ds(ss * T, T), a_cols(i)]

    def a_begin(i):
        src = acts.at[:, :, a_cols(i)]
        for q in range(2, seq, 2):
            go(src, a_at(s, i), a_send.at[i, q // 2], a_recv.at[i, q // 2], (d, xor(s, q)))
        go(src, a_at(s, i), f_send.at[i, 0], f_recv.at[i, 0], (d, flip(s, 1)))

    def a_forward(i):
        for q in range(2, seq, 2):
            here = a_at(xor(s, q), i)
            landed(here, a_recv.at[i, q // 2], d, s).wait_recv()
            go(here, here, f_send.at[i, q // 2], f_recv.at[i, q // 2], (d, flip(s, 1)))

    def a_finish(i):
        for q in range(0, seq, 2):
            landed(a_at(flip(xor(s, q), 1), i), f_recv.at[i, q // 2], d, s).wait_recv()

    def g_cols(ss, ll):
        return pl.ds(pl.multiple_of((ss * L + ll) * nb, 128), nb)

    def b_at(ss, j):
        return b_own.at[:, pl.ds(ss * T, T), pl.ds(pl.multiple_of(xor(l, j) * nb, 128), nb)]

    def b_out(ll, ss):
        return b_all.at[pl.ds(ll * E, E), pl.ds(ss * T, T), :]

    def b_begin(j):
        for q in reversed(range(1, seq)):
            ss = xor(s, q)
            go(grads.at[:, :, g_cols(ss, xor(l, j))], b_at(s, j),
               b1_send.at[q, j], b1_recv.at[q, j], (d, ss))

    def b_forward(q, j):
        ss = xor(s, q)
        if q:
            landed(b_at(ss, j), b1_recv.at[q, j], d, s).wait_recv()
        if j:
            src = b_at(ss, j) if q else grads.at[:, :, g_cols(s, xor(l, j))]
            go(src, b_out(l, ss), b2_send.at[q, j], b2_recv.at[q, j], (h * L + xor(l, j), s))

    a_begin(0)
    owns = [
        pltpu.make_async_copy(acts, a_own.at[:, pl.ds(s * T, T), :], own_sem.at[0]),
        pltpu.make_async_copy(
            grads.at[:, :, pl.ds(pl.multiple_of(s * L * nb, 128), L * nb)],
            b_own.at[:, pl.ds(s * T, T), :], own_sem.at[1]),
    ]
    for copy in owns:
        copy.start()
    for j in reversed(range(1, L)):
        b_begin(j)
        b_forward(0, j)
    b_begin(0)
    for i in range(1, len(tiles)):
        a_begin(i)
    a_forward(0)
    a_finish(0)
    for copy in owns:
        copy.wait()
    spread = Spread(h, l, s, L, lambda e: a_own.at[e, :, a_cols(0)], a_first,
                    (t_send, t_recv, tf_send, tf_recv, local_sem), copies)
    spread.begin()
    for j in reversed(range(1, L)):
        for q in range(1, seq):
            b_forward(q, j)
    spread.forward()
    for q in range(1, seq):
        b_forward(q, 0)
    mine = pltpu.make_async_copy(
        b_own.at[:, :, pl.ds(pl.multiple_of(l * nb, 128), nb)], b_all.at[pl.ds(l * E, E)], own_sem.at[2])
    mine.start()
    for i in range(1, len(tiles)):
        a_forward(i)
    for i in range(1, len(tiles)):
        a_finish(i)
    spread.finish()
    for j in range(1, L):
        for q in range(seq):
            landed(b_out(xor(l, j), xor(s, q)), b2_recv.at[q, j], d, s).wait_recv()
    mine.wait()
    for copy in copies:
        copy.wait_send()


def gather(dp, seq, L, acts, grads):
    E, T, D = acts.shape
    nb = grads.shape[2] // (seq * L)
    H, RB = dp // L, D // dp
    TM = math.lcm(RB, 128)
    tiles = D // TM
    dma = pltpu.SemaphoreType.DMA
    shape = lambda *sizes: jax.ShapeDtypeStruct(sizes, jnp.bfloat16)
    return pl.pallas_call(
        functools.partial(gather_kernel, H, L, seq, RB, TM),
        out_shape=(shape(E, seq * T, D), shape(L * E, seq * T, TM),
                   shape(E, seq * T, L * nb), shape(L * E, seq * T, nb)),
        in_specs=[pl.BlockSpec(memory_space=pl.ANY)] * 2,
        out_specs=(pl.BlockSpec(memory_space=pl.ANY),) * 4,
        scratch_shapes=[dma((tiles, seq // 2))] * 4 + [dma((seq, L))] * 4 + [dma((L,))] * 4
        + [dma((2,)), dma((3,))],
        compiler_params=pltpu.CompilerParams(collective_id=0, has_side_effects=True),
        name="gather_tokens",
    )(acts, grads)


def product_kernel(H, L, seq, RB, TM, factor, part, a_own, a_first, b_ref, out, norms, a_rest,
                   a_buf, b_buf, c_buf, recv, slots, n_send, n_recv, t_send, t_recv, tf_send, tf_recv,
                   local_sem, a_sem, b_sem, s_send, s_recv, o_send, o_recv, own_sem):
    d, s = lax.axis_index("dp"), lax.axis_index("seq")
    h, l = d // L, d % L
    D = a_own.shape[2]
    examples, tokens, nb = b_ref.shape
    tiles, k = D // TM, TM // RB
    order = steps_of(H, L, RB, TM, D, h)
    b_load = pltpu.make_async_copy(b_ref, b_buf, b_sem)
    b_load.start()

    def a_load(i):
        src = a_first if i == 0 else a_rest.at[i - 1]
        return pltpu.make_async_copy(src, a_buf.at[i % 2], a_sem.at[i % 2])

    a_load(0).start()
    group = [(j, q) for j in range(L) for q in range(seq) if j or q]
    barrier = pltpu.get_barrier_semaphore()
    for o in range(1, H):
        pl.semaphore_signal(barrier, inc=1, device_id=((h + o) % H * L + l, s), device_id_type=MESH)
    for j, q in group:
        pl.semaphore_signal(barrier, inc=1, device_id=(h * L + xor(l, j), xor(s, q)), device_id_type=MESH)
    pl.semaphore_wait(barrier, H - 1 + len(group))

    copies = []
    for j, q in group:
        copy = pltpu.make_async_remote_copy(
            src_ref=part, dst_ref=slots.at[l * seq + s],
            send_sem=n_send.at[j, q], recv_sem=n_recv.at[j, q],
            device_id=(h * L + xor(l, j), xor(s, q)), device_id_type=MESH)
        copy.start()
        copies.append(copy)
    slots[l * seq + s] = part[...]

    def spread_of(i):
        column = pl.ds(pl.multiple_of(order[i] * TM, 128), TM)
        return Spread(h, l, s, L, lambda e: a_own.at[e, :, column], a_rest.at[i - 1],
                      tuple(x.at[i - 1] for x in (t_send, t_recv, tf_send, tf_recv, local_sem)), copies)

    spreads = [None] + [spread_of(i) for i in range(1, tiles)]
    for spread in spreads[1:]:
        spread.begin()

    for j, q in group:
        landed(slots.at[xor(l, j) * seq + xor(s, q)], n_recv.at[j, q], d, s).wait_recv()
    b_load.wait()
    part_rows = 64
    for ll in range(L):
        total = slots[ll * seq]
        for ss in range(1, seq):
            total = total + slots[ll * seq + ss]
        norm = jnp.sqrt(total)
        norms[ll] = norm
        scale = jnp.minimum(1.0, 1.0 / (norm + 1e-06)) * factor
        for e in range(2):
            one = scale[e:e + 1, 0:1]

            @pl.loop(0, tokens // part_rows)
            def _(m):
                rows = pl.ds(pl.multiple_of(m * part_rows, part_rows), part_rows)
                value = b_buf[2 * ll + e, rows, :].astype(jnp.float32) * one
                b_buf[2 * ll + e, rows, :] = value.astype(jnp.bfloat16)

    def s_copy(block):
        hh, ll = block // L, block % L
        slot = (h - hh + H) % H - 1
        return pltpu.make_async_remote_copy(
            src_ref=c_buf.at[pl.ds(pl.multiple_of(block * RB, 16), RB)],
            dst_ref=recv.at[slot, pl.ds(pl.multiple_of(ll * RB, 16), RB)],
            send_sem=s_send.at[block], recv_sem=s_recv.at[slot, ll],
            device_id=(hh * L + l, s), device_id_type=MESH)

    chunk = 384
    for i, tile in enumerate(order):
        if i:
            spreads[i].finish()
            a_load(i).start()
        a_load(i).wait()

        @pl.loop(0, TM // chunk)
        def _(m):
            column = pl.multiple_of(m * chunk, 128)
            left = a_buf[i % 2, :, :, pl.ds(column, chunk)].reshape(examples * tokens, chunk)
            value = lax.dot_general(
                left, b_buf[...].reshape(examples * tokens, nb),
                (((0,), (0,)), ((), ())), preferred_element_type=jnp.float32)
            row = pl.multiple_of(tile * TM + m * chunk, 128)
            c_buf[pl.ds(row, chunk), :] = value.astype(jnp.bfloat16)

        for j in range(k):
            block = tile * k + j
            if L % k == 0:
                if i < tiles - L // k:
                    s_copy(block).start()
            else:
                @pl.when(block // L != h)
                def _():
                    s_copy(block).start()
        if i + 1 < tiles:
            spreads[i + 1].forward()

    def o_copy(ll):
        src = c_buf.at[pl.ds(pl.multiple_of((h * L + ll) * RB, 16), RB)]
        return pltpu.make_async_remote_copy(
            src_ref=src, dst_ref=out.at[:, pl.ds(pl.multiple_of(l * nb, 128), nb)],
            send_sem=o_send.at[ll], recv_sem=o_recv.at[l],
            device_id=(h * L + ll, s), device_id_type=MESH)

    own = pltpu.make_async_copy(
        c_buf.at[pl.ds(pl.multiple_of((h * L + l) * RB, 16), RB)],
        out.at[:, pl.ds(pl.multiple_of(l * nb, 128), nb)], own_sem)
    step = 96
    for ll in range(L):
        for slot in range(H - 1):
            landed(recv.at[slot, pl.ds(ll * RB, RB)], s_recv.at[slot, ll], d, s).wait_recv()

        @pl.loop(0, RB // step)
        def _(m):
            here = pl.ds(pl.multiple_of((h * L + ll) * RB + m * step, 16), step)
            there = pl.ds(pl.multiple_of(ll * RB + m * step, 16), step)
            total = c_buf[here, :].astype(jnp.float32)
            for slot in range(H - 1):
                total = total + recv[slot, there, :].astype(jnp.float32)
            c_buf[here, :] = total.astype(jnp.bfloat16)

        @pl.when(l != ll)
        def _():
            o_copy(ll).start()

        @pl.when(l == ll)
        def _():
            own.start()
    for o in range(1, H):
        for ll in range(L):
            s_copy((h + o) % H * L + ll).wait_send()
    for j in range(1, L):
        ll = xor(l, j)
        land = out.at[:, pl.ds(pl.multiple_of(ll * nb, 128), nb)]
        landed(land, o_recv.at[ll], d, s).wait_recv()
        o_copy(ll).wait_send()
    own.wait()
    for copy in copies:
        copy.wait_send()


def product(dp, seq, L, factor, part, a_own, a_first, b_all):
    examples, tokens, nb = b_all.shape
    D = a_own.shape[2]
    H, RB = dp // L, D // dp
    TM = math.lcm(RB, 128)
    rest = D // TM - 1
    dma = pltpu.SemaphoreType.DMA
    vmem, anywhere = pl.BlockSpec(memory_space=pltpu.VMEM), pl.BlockSpec(memory_space=pl.ANY)
    return pl.pallas_call(
        functools.partial(product_kernel, H, L, seq, RB, TM, factor),
        out_shape=(
            jax.ShapeDtypeStruct((RB, nb * L), jnp.bfloat16),
            jax.ShapeDtypeStruct((L, 8, 128), jnp.float32),
            jax.ShapeDtypeStruct((rest, examples, tokens, TM), jnp.bfloat16),
        ),
        in_specs=[vmem, anywhere, anywhere, anywhere],
        out_specs=(anywhere, vmem, anywhere),
        scratch_shapes=[
            pltpu.VMEM((2, examples, tokens, TM), jnp.bfloat16),
            pltpu.VMEM((examples, tokens, nb), jnp.bfloat16),
            pltpu.VMEM((D, nb), jnp.bfloat16),
            pltpu.VMEM((H - 1, L * RB, nb), jnp.bfloat16),
            pltpu.VMEM((L * seq, 8, 128), jnp.float32),
            dma((L, seq)), dma((L, seq)),
            dma((rest, L)), dma((rest, L)), dma((rest, L)), dma((rest, L)), dma((rest, 2)),
            dma((2,)), dma, dma((dp,)), dma((H - 1, L)), dma((L,)), dma((L,)), dma,
        ],
        compiler_params=pltpu.CompilerParams(
            collective_id=1, has_side_effects=True, vmem_limit_bytes=60 * 2**20),
        cost_estimate=pl.CostEstimate(
            flops=2 * examples * tokens * D * nb,
            bytes_accessed=2 * (examples * tokens * (D + nb) + RB * nb * L), transcendentals=0),
        name="product_scatter",
    )(part, a_own, a_first, b_all)


def on_device(acts, grads):
    seq, dp = lax.axis_size("seq"), lax.axis_size("dp")
    examples, local_len, width = acts.shape
    hidden = grads.shape[2]
    L = split_of(dp, seq, hidden)
    a_own, a_first, b_own, b_all = gather(dp, seq, L, acts, grads)
    act_gram = jnp.einsum("nih,nfh->nif", a_own, a_own, preferred_element_type=jnp.float32)
    grad_gram = jnp.einsum("nih,nfh->nif", b_own, b_own, preferred_element_type=jnp.float32)
    part = jnp.sum(act_gram * grad_gram, axis=(1, 2))
    tile = jnp.pad(jnp.broadcast_to(part[:, None], (examples, 128)), ((0, 8 - examples), (0, 0)))
    factor = math.sqrt(width * hidden / (examples * dp))
    update, norms, _ = product(dp, seq, L, factor, tile, a_own, a_first, b_all)
    own = lax.dynamic_slice(norms, (lax.axis_index("dp") % L, 0, 0), (1, examples, 1))
    return update, own.reshape(examples)


def solution(mesh):
    return jax.shard_map(
        on_device,
        mesh=mesh,
        in_specs=(P("dp", "seq", None), P("dp", "seq", None)),
        out_specs=(P("dp", "seq"), P("dp")),
        check_vma=False,
    )
```

time: 1010 us -> 742 us (0.73)
  Pallas kernels: 0 us -> 716 us
  waiting for transfers between devices: 675 us -> 0 us
  blocking collectives: 150 us -> 0 us
  local copies, waits for them, and re-layouts: 102 us -> 7.2 us
  matrix products: 69.6 us -> 15.9 us
  between operations: 14.1 us -> 0.69 us
    pallas_call x0 -> x2, Pallas kernels: none -> 716 us  [the longest x1 378 us: product(): pl.pallas_call(functools.partial(product_kernel, H, L, seq, RB, TM, facto...]
    unnamed x3 -> x0, waiting for transfers between devices: 675 us -> none
    all_to_all x1 -> x0, blocking collectives: 144 us -> none  [on_device(): lax.all_to_all(grads, 'seq', split_axis=2, concat_axis=1, tiled=True)]
    unnamed x4 -> x3, local copies, waits for them, and re-layouts: 78.6 us -> 5.23 us
    dot_general x3 -> x2, matrix products: 69.6 us -> 15.9 us  [the longest x1 10.5 us: on_device(): jnp.einsum('nih,nfh->nif', a_own, a_own, preferred_element_type=jnp.float32)]
    all_to_all x1 -> x0, local copies, waits for them, and re-layouts: 23.8 us -> none  [on_device(): lax.all_to_all(grads, 'seq', split_axis=2, concat_axis=1, tiled=True)]
  transfers between devices with their start and end apart: 2 -> 0, of which waited for: 1 -> 0; matrix products, arithmetic and copies ran while one was open for 5% -> 0% of each run, Pallas kernels for 0% -> 0%
where the time goes in v2:
time: 742 us; the launch traced here: 739 us
  Pallas kernels  716 us (96%)
  matrix products  15.9 us (2%)
    pallas_call x1, Pallas kernels, product(): pl.pallas_call(functools.partial(product_kernel, H, L, seq, RB, TM, facto...  378 us
    pallas_call x1, Pallas kernels, gather(): pl.pallas_call(functools.partial(gather_kernel, H, L, seq, RB, TM), out_s...  337 us

profile of v2, /device:TPU:0, one launch (start us, length us, event | category | flops | bytes accessed | tf_op | source)
XLA Modules:
  0.0 739.3 jit_solution(2864054292320613780)
XLA Ops:
  0.6 337.4 %gather_tokens.1 = (bf16[2,512,4608]{2,1,0:T(8,128)(2,1)}, bf16[8,512,1152]{2,1,0:T(8,128)(2,1)}, bf16[2,512,4608]{2,1,0:T(8,128)(2,1)}, bf16[8,512,1152]{2,1,0:T(8,128)(2,1)}) custom-call(bf16[2,128,4608]{2,1,0:T(8,128)(2,1)} %acts.1, bf16[2,128,18432]{2,1,0:T(8,128)(2,1)} %grads.1), custom_call_target="tpu_custom_call" | custom-call | tf_op jit(solution)/shard_map/gather_tokens/pallas_call | solution.py:224
  338.0 0.0 copy-start
  338.1 10.5 %fusion = f32[2,512,512]{2,1,0:T(8,128)S(1)} fusion(bf16[2,512,4608]{2,1,0:T(8,128)(2,1)} %get-tuple-element.8.a_own), kind=kOutput, calls=%fused_computation.2 | convolution fusion | flops 4831838208 | bytes 11534336 | tf_op jit(solution)/shard_map/nih,nfh->nif/dot_general | solution.py:425
  348.6 0.0 copy-done
  348.6 5.3 multiply_reduce_fusion
  353.9 0.7 pad.7.part
  354.6 378.1 %product_scatter.1 = (bf16[576,4608]{1,0:T(8,128)(2,1)}, f32[4,8,128]{2,1,0:T(8,128)}, bf16[3,8,512,1152]{3,2,1,0:T(8,128)(2,1)}) custom-call(f32[8,128]{1,0:T(8,128)} %pad.7.part, bf16[2,512,4608]{2,1,0:T(8,128)(2,1)} %get-tuple-element.8.a_own, bf16[8,512,1152]{2,1,0:T(8,128)(2,1)} %get-tuple-element.10.a_first, bf16[8,512,1152]{2,1,0:T(8,128)(2,1)} %get-tuple-element.11.b_ref), custom_call_target="tpu_custom_call" | custom-call | flops 43486543872 | bytes 52494336 | tf_op jit(solution)/shard_map/product_scatter/pallas_call | solution.py:391
  732.7 1.3 dynamic-slice_reduce_fusion
  734.0 5.2 copy.5
  (1 shorter events, 0.0 us)
Async XLA Ops:
  338.0 10.6 %copy-start = (bf16[2,512,4608]{2,1,0:T(8,128)(2,1)S(1)}, bf16[2,512,4608]{2,1,0:T(8,128)(2,1)}, u32[]{:S(2)}) copy-start(bf16[2,512,4608]{2,1,0:T(8,128)(2,1)} %get-tuple-element.9) | copy-start | bytes 28311556

commit v3 on v1

--- a/solution.py
+++ b/solution.py
@@ -188,58 +188,89 @@
     )(acts, grads)
 
 
-def product_kernel(H, L, RB, TM, a_ref, b_ref, out, a_buf, b_buf, c_buf, recv,
+def landed_copy(ref, sem, d, s):
+    return pltpu.make_async_remote_copy(
+        src_ref=ref, dst_ref=ref, send_sem=sem, recv_sem=sem, device_id=(d, s), device_id_type=MESH)
+
+
+CUTS = 3
+
+
+def product_kernel(H, L, seq, RB, TM, factor, part, a_ref, b_ref, out, norms,
+                   a_buf, b_buf, c_buf, recv, slots, n_send, n_recv,
                    a_sem, b_sem, s_send, s_recv, o_send, o_recv, own_sem):
     d, s = lax.axis_index("dp"), lax.axis_index("seq")
     h, l = d // L, d % L
     K, D = a_ref.shape
     nb = b_ref.shape[1]
-    tiles, k = D // TM, TM // RB
+    tiles, k, sub = D // TM, TM // RB, RB // CUTS
+    whole_tiles = L % k == 0
     b_load = pltpu.make_async_copy(b_ref, b_buf, b_sem)
     b_load.start()
-    whole_tiles = L % k == 0
-    plan = []
     if whole_tiles:
         per = L // k
-        for o in list(range(1, H)) + [0]:
-            hh = (h + o) % H
-            for i in reversed(range(per)):
-                tile = hh * per + xor(l // k, i)
-                plan.append((tile, [(tile * k + xor(l % k, j), o != 0) for j in reversed(range(k))]))
+        order = [((h + o) % H * per + xor(l // k, i), o != 0)
+                 for o in list(range(1, H)) + [0] for i in reversed(range(per))]
     else:
-        first = (h + 1) * L // k
-        for i in range(tiles):
-            tile = (first + i) % tiles
-            plan.append((tile, [(tile * k + j, None) for j in range(k)]))
+        order = [(((h + 1) * L // k + i) % tiles, None) for i in range(tiles)]
 
     def a_load(i):
-        column = pl.multiple_of(plan[i][0] * TM, 128)
+        column = pl.multiple_of(order[i][0] * TM, 128)
         return pltpu.make_async_copy(a_ref.at[:, pl.ds(column, TM)], a_buf.at[i % 2], a_sem.at[i % 2])
 
     a_load(0).start()
+    group = [(j, q) for j in range(L) for q in range(seq) if j or q]
     barrier = pltpu.get_barrier_semaphore()
     for o in range(1, H):
         pl.semaphore_signal(barrier, inc=1, device_id=((h + o) % H * L + l, s), device_id_type=MESH)
-    for i in range(1, L):
-        pl.semaphore_signal(barrier, inc=1, device_id=(h * L + xor(l, i), s), device_id_type=MESH)
-    pl.semaphore_wait(barrier, H + L - 2)
-
-    def s_copy(block):
+    for j, q in group:
+        pl.semaphore_signal(barrier, inc=1, device_id=(h * L + xor(l, j), xor(s, q)), device_id_type=MESH)
+    pl.semaphore_wait(barrier, H - 1 + len(group))
+
+    def n_copy(j, q):
+        return pltpu.make_async_remote_copy(
+            src_ref=part, dst_ref=slots.at[l * seq + s],
+            send_sem=n_send.at[j, q], recv_sem=n_recv.at[j, q],
+            device_id=(h * L + xor(l, j), xor(s, q)), device_id_type=MESH)
+
+    for j, q in group:
+        n_copy(j, q).start()
+    slots[l * seq + s] = part[...]
+    for j, q in group:
+        landed_copy(slots.at[xor(l, j) * seq + xor(s, q)], n_recv.at[j, q], d, s).wait_recv()
+    total = slots[0]
+    for j in range(1, L * seq):
+        total = total + slots[j]
+    norm = jnp.sqrt(total)
+    norms[...] = norm
+    scale = jnp.minimum(1.0, 1.0 / (norm + 1e-06)) * factor
+    b_load.wait()
+    some = 64
+    tokens = K // (2 * L)
+    for e in range(2 * L):
+        one = scale[e:e + 1, 0:1]
+
+        @pl.loop(0, tokens // some)
+        def _(m):
+            rows = pl.ds(pl.multiple_of(e * tokens + m * some, some), some)
+            b_buf[rows, :] = (b_buf[rows, :].astype(jnp.float32) * one).astype(jnp.bfloat16)
+
+    def s_copy(piece):
+        block = piece // CUTS
         hh, ll = block // L, block % L
         slot = (h - hh + H) % H - 1
-        return pltpu.make_async_remote_copy(
-            src_ref=c_buf.at[pl.ds(pl.multiple_of(block * RB, 16), RB)],
-            dst_ref=recv.at[slot, pl.ds(pl.multiple_of(ll * RB, 16), RB)],
-            send_sem=s_send.at[block], recv_sem=s_recv.at[slot, ll],
+        place = ll * CUTS + piece % CUTS
+        return pltpu.make_async_remote_copy(
+            src_ref=c_buf.at[pl.ds(pl.multiple_of(piece * sub, 16), sub)],
+            dst_ref=recv.at[slot, pl.ds(pl.multiple_of(place * sub, 16), sub)],
+            send_sem=s_send.at[piece], recv_sem=s_recv.at[slot, place],
             device_id=(hh * L + l, s), device_id_type=MESH)
 
     chunk = 384
-    for i, (tile, rows) in enumerate(plan):
+    for i, (tile, away) in enumerate(order):
         if i + 1 < tiles:
             a_load(i + 1).start()
         a_load(i).wait()
-        if i == 0:
-            b_load.wait()
 
         @pl.loop(0, TM // chunk)
         def _(m):
@@ -249,84 +280,103 @@
                 (((0,), (0,)), ((), ())), preferred_element_type=jnp.float32)
             row = pl.multiple_of(tile * TM + m * chunk, 128)
             c_buf[pl.ds(row, chunk), :] = value.astype(jnp.bfloat16)
-
-        for block, away in rows:
-            if away is None:
-                @pl.when(block // L != h)
-                def _():
-                    s_copy(block).start()
-            elif away:
-                s_copy(block).start()
-
-    def o_copy(i):
-        ll = xor(l, i)
-        src = c_buf.at[pl.ds(pl.multiple_of((h * L + ll) * RB, 16), RB)]
-        return pltpu.make_async_remote_copy(
-            src_ref=src, dst_ref=out.at[:, pl.ds(pl.multiple_of(l * nb, 128), nb)],
-            send_sem=o_send.at[i], recv_sem=o_recv.at[i],
+            for u in range(chunk // sub):
+                piece = tile * (TM // sub) + m * (chunk // sub) + u
+                if away is None:
+                    @pl.when(piece // (CUTS * L) != h)
+                    def _():
+                        s_copy(piece).start()
+                elif away:
+                    s_copy(piece).start()
+
+    def c_rows(place):
+        return c_buf.at[pl.ds(pl.multiple_of((h * L * CUTS + place) * sub, 16), sub)]
+
+    def o_copy(place):
+        ll, u = place // CUTS, place % CUTS
+        return pltpu.make_async_remote_copy(
+            src_ref=c_rows(place),
+            dst_ref=out.at[pl.ds(pl.multiple_of(u * sub, 16), sub), pl.ds(pl.multiple_of(l * nb, 128), nb)],
+            send_sem=o_send.at[place], recv_sem=o_recv.at[l, u],
             device_id=(h * L + ll, s), device_id_type=MESH)
 
-    own = pltpu.make_async_copy(
-        c_buf.at[pl.ds(pl.multiple_of((h * L + l) * RB, 16), RB)],
-        out.at[:, pl.ds(pl.multiple_of(l * nb, 128), nb)], own_sem)
+    def own(u):
+        return pltpu.make_async_copy(
+            c_rows(l * CUTS + u),
+            out.at[pl.ds(u * sub, sub), pl.ds(pl.multiple_of(l * nb, 128), nb)], own_sem.at[u])
+
+    if whole_tiles:
+        places = [xor(l // k, i) * k * CUTS + j for i in reversed(range(per)) for j in range(k * CUTS)]
+    else:
+        places = list(range(L * CUTS))
     step = 96
-    for i in reversed(range(L)):
-        ll = xor(l, i)
+    for at, place in enumerate(places):
         for slot in range(H - 1):
-            land = recv.at[slot, pl.ds(pl.multiple_of(ll * RB, 16), RB)]
-            pltpu.make_async_remote_copy(
-                src_ref=land, dst_ref=land, send_sem=s_recv.at[slot, ll],
-                recv_sem=s_recv.at[slot, ll], device_id=(d, s), device_id_type=MESH).wait_recv()
-
-        @pl.loop(0, RB // step)
+            land = recv.at[slot, pl.ds(pl.multiple_of(place * sub, 16), sub)]
+            landed_copy(land, s_recv.at[slot, place], d, s).wait_recv()
+
+        @pl.loop(0, sub // step)
         def _(m):
-            here = pl.ds(pl.multiple_of((h * L + ll) * RB + m * step, 16), step)
-            there = pl.ds(pl.multiple_of(ll * RB + m * step, 16), step)
-            total = c_buf[here, :].astype(jnp.float32)
+            here = pl.ds(pl.multiple_of((h * L * CUTS + place) * sub + m * step, 16), step)
+            there = pl.ds(pl.multiple_of(place * sub + m * step, 16), step)
+            value = c_buf[here, :].astype(jnp.float32)
             for slot in range(H - 1):
-                total = total + recv[slot, there, :].astype(jnp.float32)
-            c_buf[here, :] = total.astype(jnp.bfloat16)
-
-        if i:
-            o_copy(i).start()
-        else:
-            own.start()
+                value = value + recv[slot, there, :].astype(jnp.float32)
+            c_buf[here, :] = value.astype(jnp.bfloat16)
+
+        @pl.when(place // CUTS != l)
+        def _():
+            o_copy(place).start()
+
+        @pl.when(place // CUTS == l)
+        def _():
+            own(at % CUTS).start()
+    for j, q in group:
+        n_copy(j, q).wait_send()
     for o in range(1, H):
-        for ll in range(L):
-            s_copy((h + o) % H * L + ll).wait_send()
-    for i in range(1, L):
-        land = out.at[:, pl.ds(pl.multiple_of(xor(l, i) * nb, 128), nb)]
-        pltpu.make_async_remote_copy(
-            src_ref=land, dst_ref=land, send_sem=o_recv.at[i], recv_sem=o_recv.at[i],
-            device_id=(d, s), device_id_type=MESH).wait_recv()
-        o_copy(i).wait_send()
-    own.wait()
-
-
-def product(dp, seq, L, a_all, b_all):
+        for place in range(L * CUTS):
+            s_copy((h + o) % H * L * CUTS + place).wait_send()
+    for j in range(1, L):
+        ll = xor(l, j)
+        for u in range(CUTS):
+            land = out.at[pl.ds(u * sub, sub), pl.ds(pl.multiple_of(ll * nb, 128), nb)]
+            landed_copy(land, o_recv.at[ll, u], d, s).wait_recv()
+            o_copy(ll * CUTS + u).wait_send()
+    for u in range(CUTS):
+        own(u).wait()
+
+
+def product(dp, seq, L, factor, part, a_all, b_all):
     K, D = a_all.shape
     nb = b_all.shape[1]
     H, RB = dp // L, D // dp
     TM = math.lcm(RB, 128)
     dma = pltpu.SemaphoreType.DMA
+    vmem, anywhere = pl.BlockSpec(memory_space=pltpu.VMEM), pl.BlockSpec(memory_space=pl.ANY)
     return pl.pallas_call(
-        functools.partial(product_kernel, H, L, RB, TM),
-        out_shape=jax.ShapeDtypeStruct((RB, nb * L), jnp.bfloat16),
-        in_specs=[pl.BlockSpec(memory_space=pl.ANY)] * 2,
-        out_specs=pl.BlockSpec(memory_space=pl.ANY),
+        functools.partial(product_kernel, H, L, seq, RB, TM, factor),
+        out_shape=(
+            jax.ShapeDtypeStruct((RB, nb * L), jnp.bfloat16),
+            jax.ShapeDtypeStruct(part.shape, jnp.float32),
+        ),
+        in_specs=[vmem, anywhere, anywhere],
+        out_specs=(anywhere, vmem),
         scratch_shapes=[
             pltpu.VMEM((2, K, TM), jnp.bfloat16),
             pltpu.VMEM((K, nb), jnp.bfloat16),
             pltpu.VMEM((D, nb), jnp.bfloat16),
             pltpu.VMEM((H - 1, L * RB, nb), jnp.bfloat16),
-            dma((2,)), dma, dma((dp,)), dma((H - 1, L)), dma((L,)), dma((L,)), dma,
+            pltpu.VMEM((L * seq,) + part.shape, jnp.float32),
+            dma((L, seq)), dma((L, seq)),
+            dma((2,)), dma, dma((dp * CUTS,)), dma((H - 1, L * CUTS)),
+            dma((L * CUTS,)), dma((L, CUTS)), dma((CUTS,)),
         ],
         compiler_params=pltpu.CompilerParams(
             collective_id=1, has_side_effects=True, vmem_limit_bytes=60 * 2**20),
         cost_estimate=pl.CostEstimate(
             flops=2 * K * D * nb, bytes_accessed=2 * (K * D + K * nb + RB * nb * L), transcendentals=0),
         name="product_scatter",
-    )(a_all, b_all)
+    )(part, a_all, b_all)
 
 
 def on_device(acts, grads):
@@ -334,21 +384,19 @@
     examples, local_len, width = acts.shape
     hidden = grads.shape[2]
     L = split_of(dp, seq, hidden)
-    d = lax.axis_index("dp")
     a_all, b_all = gather(L, seq, acts, grads)
     act_gram = jnp.einsum("nih,nfh->nif", a_all, a_all, preferred_element_type=jnp.float32)
     grad_gram = jnp.einsum("nih,nfh->nif", b_all, b_all, preferred_element_type=jnp.float32)
+    act_gram, grad_gram = lax.optimization_barrier((act_gram, grad_gram))
     part = jnp.sum(act_gram * grad_gram, axis=(1, 2))
-    here = d // L * (L * examples)
-    every = lax.dynamic_update_slice(jnp.zeros((dp * examples,), jnp.float32), part, (here,))
-    norms = jnp.sqrt(lax.psum(every, ("dp", "seq")))
-    clip = jnp.minimum(1.0, 1.0 / (norms + 1e-06))
+    rows = -(-L * examples // 8) * 8
+    tile = jnp.pad(jnp.broadcast_to(part[:, None], (L * examples, 128)), ((0, rows - L * examples), (0, 0)))
     factor = math.sqrt(width * hidden / (examples * dp))
-    scale = lax.dynamic_slice(clip * factor, (here,), (L * examples,))
-    scaled = (b_all * scale[:, None, None]).astype(jnp.bfloat16)
     tokens = L * examples * seq * local_len
-    update = product(dp, seq, L, a_all.reshape(tokens, width), scaled.reshape(tokens, -1))
-    return update, lax.dynamic_slice(norms, (d * examples,), (examples,))
+    update, norms = product(
+        dp, seq, L, factor, tile, a_all.reshape(tokens, width), b_all.reshape(tokens, -1))
+    own = lax.dynamic_slice(norms, (lax.axis_index("dp") % L * examples, 0), (examples, 1))
+    return update, own.reshape(examples)
 
 
 def solution(mesh):

time: 596 us -> 558 us (0.936)
  blocking collectives: 39.6 us -> 0 us
    psum x1 -> x0, blocking collectives: 39.6 us -> none  [on_device(): norms = jnp.sqrt(lax.psum(every, ('dp', 'seq')))]
    convert_element_type x1 -> x0, other arithmetic: 9.86 us -> none  [on_device(): scaled = (b_all * scale[:, None, None]).astype(jnp.bfloat16)]
where the time goes in v3:
time: 558 us; the launch traced here: 557 us
  Pallas kernels  499 us (89%)
  matrix products  45.6 us (8%)
  local copies, waits for them, and re-layouts  7.19 us (1%)
    pallas_call x1, Pallas kernels, product(): pl.pallas_call(functools.partial(product_kernel, H, L, seq, RB, TM, facto...  257 us
    pallas_call x1, Pallas kernels, gather(): pl.pallas_call(functools.partial(gather_kernel, L, seq), out_shape=(jax.S...  243 us
    dot_general x1, matrix products, on_device(): jnp.einsum('nih,nfh->nif', a_all, a_all, preferred_element_type=jnp.float32)  32.5 us
    dot_general x1, matrix products, on_device(): jnp.einsum('nih,nfh->nif', b_all, b_all, preferred_element_type=jnp.float32)  13.1 us

profile of v3, /device:TPU:0, one launch (start us, length us, event | category | flops | bytes accessed | tf_op | source)
XLA Modules:
  0.0 557.3 jit_solution(11378805982261670163)
XLA Ops:
  0.6 242.7 %gather_tokens.1 = (bf16[8,512,4608]{2,1,0:T(8,128)(2,1)}, bf16[8,512,1152]{2,1,0:T(8,128)(2,1)}) custom-call(bf16[2,128,4608]{2,1,0:T(8,128)(2,1)} %acts.1, bf16[2,128,18432]{2,1,0:T(8,128)(2,1)} %grads.1), custom_call_target="tpu_custom_call" | custom-call | tf_op jit(solution)/shard_map/gather_tokens/pallas_call | solution.py:173
  243.3 32.5 %fusion = f32[8,512,512]{2,1,0:T(8,128)} fusion(bf16[8,512,4608]{2,1,0:T(8,128)(2,1)} %get-tuple-element.8), kind=kOutput, calls=%fused_computation.2 | convolution fusion | flops 19327352832 | bytes 46137344 | tf_op jit(solution)/shard_map/nih,nfh->nif/dot_general | solution.py:388
  275.8 0.0 copy-start
  275.8 13.1 %fusion.1 = f32[8,512,512]{2,1,0:T(8,128)} fusion(bf16[8,512,1152]{2,1,0:T(8,128)(2,1)} %get-tuple-element.9), kind=kOutput, calls=%fused_computation.3 | convolution fusion | flops 4831838208 | bytes 17825792 | tf_op jit(solution)/shard_map/nih,nfh->nif/dot_general | solution.py:389
  288.9 0.0 copy-done
  288.9 4.5 multiply_reduce_fusion
  293.4 0.7 broadcast_in_dim.2.part
  294.0 256.7 %product_scatter.1 = (bf16[576,4608]{1,0:T(8,128)(2,1)}, f32[8,128]{1,0:T(8,128)}) custom-call(f32[8,128]{1,0:T(8,128)} %broadcast_in_dim.2.part, bf16[4096,4608]{1,0:T(8,128)(2,1)} %bitcast.6, bf16[4096,1152]{1,0:T(8,128)(2,1)} %bitcast.7), custom_call_target="tpu_custom_call" | custom-call | flops 43486543872 | bytes 52494336 | tf_op jit(solution)/shard_map/product_scatter/pallas_call | solution.py:356
  550.8 1.3 dynamic-slice_reduce_fusion
  552.1 5.2 copy.5
Async XLA Ops:
  275.8 13.1 %copy-start = (f32[8,512,512]{2,1,0:T(8,128)S(1)}, f32[8,512,512]{2,1,0:T(8,128)}, u32[]{:S(2)}) copy-start(f32[8,512,512]{2,1,0:T(8,128)} %fusion) | copy-start | bytes 25165828

commit v4 on v3

--- a/solution.py
+++ b/solution.py
@@ -379,18 +379,50 @@
     )(part, a_all, b_all)
 
 
+def gram_kernel(a_ref, b_ref, out):
+    half = a_ref.shape[1] // 2
+
+    def gram(ref, i, j):
+        return lax.dot_general(
+            ref[0, i * half:(i + 1) * half, :], ref[0, j * half:(j + 1) * half, :],
+            (((1,), (1,)), ((), ())), preferred_element_type=jnp.float32)
+
+    total = jnp.zeros((half, half), jnp.float32)
+    for i, j, weight in ((0, 0, 1.0), (1, 0, 2.0), (1, 1, 1.0)):
+        total = total + weight * (gram(a_ref, i, j) * gram(b_ref, i, j))
+    whole = jnp.sum(jnp.sum(total, axis=0, keepdims=True), axis=1, keepdims=True)
+    out[0] = jnp.broadcast_to(whole, out.shape[1:])
+
+
+def squared_parts(a_all, b_all):
+    count, tokens, width = a_all.shape
+    nb = b_all.shape[2]
+    return pl.pallas_call(
+        gram_kernel,
+        grid=(count,),
+        out_shape=jax.ShapeDtypeStruct((count, 8, 128), jnp.float32),
+        in_specs=[
+            pl.BlockSpec((1, tokens, width), lambda i: (i, 0, 0)),
+            pl.BlockSpec((1, tokens, nb), lambda i: (i, 0, 0)),
+        ],
+        out_specs=pl.BlockSpec((1, 8, 128), lambda i: (i, 0, 0)),
+        compiler_params=pltpu.CompilerParams(vmem_limit_bytes=40 * 2**20),
+        cost_estimate=pl.CostEstimate(
+            flops=2 * count * tokens * tokens * (width + nb),
+            bytes_accessed=2 * count * tokens * (width + nb), transcendentals=0),
+        name="grams",
+    )(a_all, b_all)
+
+
 def on_device(acts, grads):
     seq, dp = lax.axis_size("seq"), lax.axis_size("dp")
     examples, local_len, width = acts.shape
     hidden = grads.shape[2]
     L = split_of(dp, seq, hidden)
     a_all, b_all = gather(L, seq, acts, grads)
-    act_gram = jnp.einsum("nih,nfh->nif", a_all, a_all, preferred_element_type=jnp.float32)
-    grad_gram = jnp.einsum("nih,nfh->nif", b_all, b_all, preferred_element_type=jnp.float32)
-    act_gram, grad_gram = lax.optimization_barrier((act_gram, grad_gram))
-    part = jnp.sum(act_gram * grad_gram, axis=(1, 2))
+    part = squared_parts(a_all, b_all)
     rows = -(-L * examples // 8) * 8
-    tile = jnp.pad(jnp.broadcast_to(part[:, None], (L * examples, 128)), ((0, rows - L * examples), (0, 0)))
+    tile = jnp.pad(part[:, 0, :], ((0, rows - L * examples), (0, 0)))
     factor = math.sqrt(width * hidden / (examples * dp))
     tokens = L * examples * seq * local_len
     update, norms = product(

time: 558 us -> 535 us (0.959)
  matrix products: 45.6 us -> 0 us
  Pallas kernels: 499 us -> 523 us
    dot_general x2 -> x0, matrix products: 45.6 us -> none  [the longest x1 32.5 us: on_device(): jnp.einsum('nih,nfh->nif', a_all, a_all, preferred_element_type=jnp.float32)]
    pallas_call x0 -> x1, Pallas kernels: none -> 23.6 us  [squared_parts(): pl.pallas_call(gram_kernel, grid=(count,), out_shape=jax.ShapeDtypeStruct...]
where the time goes in v4:
time: 535 us; the launch traced here: 534 us
  Pallas kernels  523 us (98%)
  local copies, waits for them, and re-layouts  10.8 us (2%)
    pallas_call x1, Pallas kernels, product(): pl.pallas_call(functools.partial(product_kernel, H, L, seq, RB, TM, facto...  257 us
    pallas_call x1, Pallas kernels, gather(): pl.pallas_call(functools.partial(gather_kernel, L, seq), out_shape=(jax.S...  243 us
    pallas_call x1, Pallas kernels, squared_parts(): pl.pallas_call(gram_kernel, grid=(count,), out_shape=jax.ShapeDtypeStruct...  23.6 us

profile of v4, /device:TPU:0, one launch (start us, length us, event | category | flops | bytes accessed | tf_op | source)
XLA Modules:
  0.0 534.4 jit_solution(3680110624480091514)
XLA Ops:
  0.6 242.7 %gather_tokens.1 = (bf16[8,512,4608]{2,1,0:T(8,128)(2,1)}, bf16[8,512,1152]{2,1,0:T(8,128)(2,1)}) custom-call(bf16[2,128,4608]{2,1,0:T(8,128)(2,1)} %acts.1, bf16[2,128,18432]{2,1,0:T(8,128)(2,1)} %grads.1), custom_call_target="tpu_custom_call" | custom-call | tf_op jit(solution)/shard_map/gather_tokens/pallas_call | solution.py:173
  243.3 0.0 copy-start
  243.3 3.7 copy-done
  247.0 23.6 %grams.1 = f32[8,8,128]{2,1,0:T(8,128)S(1)} custom-call(bf16[8,512,4608]{2,1,0:T(8,128)(2,1)} %get-tuple-element.6.a_ref, bf16[8,512,1152]{2,1,0:T(8,128)(2,1)S(1)} %copy-done), custom_call_target="tpu_custom_call" | custom-call | flops 24159191040 | bytes 47185920 | tf_op jit(solution)/shard_map/grams/pallas_call | solution.py:400
  270.5 0.6 slice.4
  271.1 256.7 %product_scatter.1 = (bf16[576,4608]{1,0:T(8,128)(2,1)}, f32[8,128]{1,0:T(8,128)}) custom-call(f32[8,128]{1,0:T(8,128)} %bitcast.6, bf16[4096,4608]{1,0:T(8,128)(2,1)} %bitcast.7, bf16[4096,1152]{1,0:T(8,128)(2,1)} %bitcast.5), custom_call_target="tpu_custom_call" | custom-call | flops 43486543872 | bytes 52494336 | tf_op jit(solution)/shard_map/product_scatter/pallas_call | solution.py:356
  527.9 1.3 dynamic-slice_reduce_fusion
  529.2 5.2 copy.8
Async XLA Ops:
  243.3 3.7 copy-start
